TPU v7x, 32 devices: a whole 2x2x4 slice. The times are simulated.
32 devices in a mesh: dp: 8 (over z, y), mp: 4 (over x, core).
Axes of the slice: x: 2, y: 2, z: 4, core: 2. Of those that a mesh axis runs over, the one named last changes fastest.
Arguments:
- features: bfloat16 [2, 2048, 1536], P(None, 'dp'), may hold values from -30 to 30
- proj_weight: bfloat16 [1536, 4096], P(None, 'mp'), may hold values from -0.15625 to 0.15625
Outputs:
- loss_value: float32 [], replicated
- feature_grad: bfloat16 [2, 2048, 1536], P(None, 'dp', 'mp')
All inputs are finite; a program needn't handle non-finite values.
Results may differ from a plain program's by a relative error of at most 0.012.
Values may be sent and summed in bfloat16 or wider, within the bound.
A program may use at most 128 MiB of HBM per device.

v0:
```python
import jax
import jax.numpy as jnp
from jax import lax
from jax.sharding import PartitionSpec as P


def on_device(features, proj_weight):
    rows = features.shape[1]
    width_loc = proj_weight.shape[1]
    n_data = lax.axis_size("dp")
    batch_all = float(rows * n_data)
    flat = features.reshape(2 * rows, features.shape[2])
    pre = jnp.dot(flat, proj_weight, preferred_element_type=jnp.float32).reshape(2, rows, width_loc)
    mean = lax.psum(jnp.sum(pre, axis=1), "dp") / batch_all
    centred = pre - mean[:, None, :]
    spread = lax.psum(jnp.sum(centred * centred, axis=1), "dp") / batch_all
    scale_inv = lax.rsqrt(spread + 1e-05)
    normed = centred * scale_inv[:, None, :]
    embed = normed.astype(jnp.bfloat16)
    view_a = embed[0]
    view_b_all = lax.all_gather(embed[1], "mp", axis=1, tiled=True)
    full_width = view_b_all.shape[1]
    own_rows = width_loc // n_data
    part_a = view_a
    corr = (
        lax.psum_scatter(
            lax.dot_general(
                part_a, view_b_all, (((0,), (0,)), ((), ())), preferred_element_type=jnp.float32
            ),
            "dp",
            scatter_dimension=0,
            tiled=True,
        )
        / batch_all
    )
    first_row = lax.axis_index("mp") * width_loc + lax.axis_index("dp") * own_rows
    row_ids = lax.broadcasted_iota(jnp.int32, (own_rows, full_width), 0) + first_row
    col_ids = lax.broadcasted_iota(jnp.int32, (own_rows, full_width), 1)
    on_diag = row_ids == col_ids
    miss = 1.0 - corr
    loss_part = jnp.sum(jnp.where(on_diag, miss * miss, 0.0051 * corr * corr))
    loss_value = lax.psum(loss_part, ("dp", "mp")) / float(full_width)
    grad_corr = jnp.where(on_diag, -2.0 * miss, 2.0 * 0.0051 * corr).astype(jnp.bfloat16)
    piece = lax.all_gather(grad_corr, "dp", axis=0, tiled=True)
    block = lax.dot_general(
        view_b_all, piece, (((1,), (1,)), ((), ())), preferred_element_type=jnp.float32
    )
    grad_a = block
    part_a = view_a
    grad_part = jnp.dot(part_a, piece, preferred_element_type=jnp.float32)
    grad_a, grad_part = (grad_a, grad_part)
    grad_b = lax.psum_scatter(
        grad_part.astype(jnp.bfloat16), "mp", scatter_dimension=1, tiled=True
    ).astype(jnp.float32)
    grads = jnp.stack([grad_a, grad_b])
    first_sum, second_sum = lax.psum(
        (jnp.sum(grads, axis=1), jnp.sum(grads * normed, axis=1)), "dp"
    )
    pre_grad = (
        scale_inv[:, None, :]
        * (grads - first_sum[:, None, :] / batch_all - normed * second_sum[:, None, :] / batch_all)
    ).astype(jnp.bfloat16)
    back = lax.dot_general(
        pre_grad.reshape(2 * rows, width_loc),
        proj_weight,
        (((1,), (1,)), ((), ())),
        preferred_element_type=jnp.float32,
    )
    summed = lax.psum_scatter(
        back.astype(jnp.bfloat16), "mp", scatter_dimension=1, tiled=True
    ).astype(jnp.float32)
    feature_grad = summed.reshape(2, rows, summed.shape[1]).astype(jnp.bfloat16)
    return (loss_value, feature_grad)


def solution(mesh):
    placed = (P(None, "dp", None), P(None, "mp"))
    return jax.shard_map(
        on_device, mesh=mesh, in_specs=placed, out_specs=(P(), P(None, "dp", "mp")), check_vma=False
    )
```

profile of v0, /device:TPU:12, one launch (start us, length us, event | category | flops | bytes accessed | tf_op | source)
XLA Modules:
  0.0 636.4 jit_solution(4720880971638177025)
XLA Ops:
  7.2 0.0 copy-start
  7.2 0.0 all-gather.6.cloned.1.call-start
  7.2 1.8 copy-done
  9.1 4.6 fusion.11
  13.6 15.4 %psum.35 = f32[2,1024]{1,0:T(2,128)S(1)} all-reduce(f32[2,1024]{1,0:T(2,128)S(1)} %get-tuple-element.8), channel_id=1, replica_groups=mesh['dp'=8,'mp'=4] {'dp'}, use_global_device_ids=true, to_apply=%region_1.0 | all-reduce | flops 2048 | bytes 16384 | tf_op jit(solution)/shard_map/psum | solution.py:14
  29.0 1.8 multiply_reduce_fusion.1
  30.9 21.6 %psum.36 = f32[2,1024]{1,0:T(2,128)S(1)} all-reduce(f32[2,1024]{1,0:T(2,128)S(1)} %multiply_reduce_fusion.1), channel_id=1, replica_groups=mesh['dp'=8,'mp'=4] {'dp'}, use_global_device_ids=true, to_apply=%region_3.0 | all-reduce | flops 2048 | bytes 16384 | tf_op jit(solution)/shard_map/psum | solution.py:16
  52.5 1.9 fusion.6
  54.4 0.0 copy-start.2
  54.4 1.0 copy-done.2
  55.4 0.8 slice.9
  56.2 0.0 all-gather.6.cloned.1.call-update
  56.2 0.0 reduce-scatter.6.cloned.1.call-start
  56.3 23.6 %all-gather.6.cloned.1.call-done = bf16[1,256,4096]{2,1,0:T(8,128)(2,1)} async-done(((bf16[1,256,1024]{2,1,0:T(8,128)(2,1)}), bf16[1,256,4096]{2,1,0:T(8,128)(2,1)}) %all-gather.6.cloned.1.call-update) | async-done | bytes 2097168 | tf_op jit(solution)/shard_map/all_gather | solution.py:21
  79.8 9.9 %fusion.4 = f32[1024,4096]{1,0:T(8,128)} fusion(bf16[1,256,4096]{2,1,0:T(8,128)(2,1)} %all-gather.6.cloned.1.call-done, bf16[2,256,1024]{2,1,0:T(8,128)(2,1)} %copy-done.2), kind=kOutput, calls=%fused_computation.7 | convolution fusion | flops 2147483648 | bytes 19398656 | tf_op jit(solution)/shard_map/dot_general | solution.py:27
  89.7 0.0 reduce-scatter.6.cloned.1.call-update
  89.7 0.0 all-gather.4.cloned.1.call-start
  89.8 280.5 %reduce-scatter.6.cloned.1.call-done = f32[128,4096]{1,0:T(8,128)} async-done(((f32[1024,4096]{1,0:T(8,128)}), f32[128,4096]{1,0:T(8,128)}) %reduce-scatter.6.cloned.1.call-update) | async-done | bytes 2097168 | tf_op jit(solution)/shard_map/reduce_scatter | solution.py:26
  370.3 4.1 select_convert_fusion
  374.4 0.0 all-gather.4.cloned.1.call-update
  374.5 0.0 reduce-scatter.8.cloned.1.call-start
  374.5 122.8 %all-gather.4.cloned.1.call-done = bf16[1024,4096]{1,0:T(8,128)(2,1)} async-done(((bf16[128,4096]{1,0:T(8,128)(2,1)}), bf16[1024,4096]{1,0:T(8,128)(2,1)}) %all-gather.4.cloned.1.call-update) | async-done | bytes 8388624 | tf_op jit(solution)/shard_map/all_gather | solution.py:44
  497.3 7.3 %convolution_convert_fusion = bf16[256,4096]{1,0:T(8,128)(2,1)} fusion(bf16[1024,4096]{1,0:T(8,128)(2,1)} %all-gather.4.cloned.1.call-done, bf16[2,256,1024]{2,1,0:T(8,128)(2,1)} %copy-done.2), kind=kOutput, calls=%fused_computation | convolution fusion | flops 2148532224 | bytes 11010048 | tf_op jit(solution)/shard_map/dot_general | solution.py:50
  504.6 0.0 reduce-scatter.8.cloned.1.call-update
  504.6 0.0 reduce-scatter.10.cloned.1.call-start
  504.7 7.4 %fusion.7 = f32[1,256,1024]{2,1,0:T(8,128)} fusion(bf16[1024,4096]{1,0:T(8,128)(2,1)} %all-gather.4.cloned.1.call-done, bf16[1,256,4096]{2,1,0:T(8,128)(2,1)} %all-gather.6.cloned.1.call-done), kind=kOutput, calls=%fused_computation.17 | convolution fusion | flops 2147483648 | bytes 11534336 | tf_op jit(solution)/shard_map/dot_general | solution.py:45
  512.0 25.2 %reduce-scatter.8.cloned.1.call-done = bf16[256,1024]{1,0:T(8,128)(2,1)} async-done(((bf16[256,4096]{1,0:T(8,128)(2,1)}), bf16[256,1024]{1,0:T(8,128)(2,1)}) %reduce-scatter.8.cloned.1.call-update) | async-done | bytes 524304 | tf_op jit(solution)/shard_map/reduce_scatter | solution.py:52
  537.3 0.0 copy-start.3
  537.3 1.2 bitcast_convert_fusion
  538.5 0.1 copy-done.3
  538.6 0.0 copy-start.1
  538.6 2.5 fusion.10
  541.1 0.0 copy-done.1
  541.2 29.9 %all-reduce = (f32[2,1024]{1,0:T(2,128)S(1)}, f32[2,1024]{1,0:T(2,128)S(1)}) all-reduce(f32[2,1024]{1,0:T(2,128)S(1)} %get-tuple-element.3, f32[2,1024]{1,0:T(2,128)S(1)} %get-tuple-element.2), channel_id=1, replica_groups=mesh['dp'=8,'mp'=4] {'dp'}, use_global_device_ids=true, to_apply=%region_11.12 | all-reduce | flops 4096 | bytes 32768 | tf_op jit(solution)/shard_map/psum | solution.py:56
  571.1 2.7 multiply_convert_fusion
  573.8 3.0 convolution_convert_fusion.1
  576.8 2.6 copy.4
  579.5 0.0 reduce-scatter.10.cloned.1.call-update
  579.5 46.6 %psum.37 = f32[]{:T(128)} all-reduce(f32[]{:T(128)} %get-tuple-element.7), channel_id=1, replica_groups=mesh['dp'=8,'mp'=4] {'dp','mp'}, use_global_device_ids=true, to_apply=%region_6.7 | all-reduce | flops 1 | bytes 8 | tf_op jit(solution)/shard_map/psum | solution.py:42
  626.8 0.0 reduce-scatter.10.cloned.1.call-done
  626.8 1.9 copy.5
  (4 shorter events, 0.0 us)
Async XLA Ops:
  7.2 1.9 copy-start
  7.2 72.7 %all-gather.6.cloned.1.call-start = ((), (), s32[]{:S(2)}) async-start(), calls=%async_computation.6 | async-start | bytes 2621440 | tf_op jit(solution)/shard_map/all_gather | solution.py:21
  54.4 1.0 copy-start.2
  56.2 314.1 %reduce-scatter.6.cloned.1.call-start = ((), (), s32[]{:S(2)}) async-start(), calls=%async_computation.3 | async-start | bytes 18874368 | tf_op jit(solution)/shard_map/reduce_scatter | solution.py:26
  89.7 407.6 %all-gather.4.cloned.1.call-start = ((), (), s32[]{:S(2)}) async-start(), calls=%async_computation.4 | async-start | bytes 9437184 | tf_op jit(solution)/shard_map/all_gather | solution.py:44
  374.5 162.8 %reduce-scatter.8.cloned.1.call-start = ((), (), s32[]{:S(2)}) async-start(), calls=%async_computation.5 | async-start | bytes 2621440 | tf_op jit(solution)/shard_map/reduce_scatter | solution.py:52
  504.6 122.2 %reduce-scatter.10.cloned.1.call-start = ((), (), s32[]{:S(2)}) async-start(), calls=%async_computation.7 | async-start | bytes 1966080
  537.3 1.4 copy-start.3
  538.6 2.5 copy-start.1
Sparse Core Ops, SparseCore 0:
  56.3 23.4 all-gather.5
  89.9 280.3 reduce-scatter.5
  374.6 122.6 all-gather.3
  504.7 32.4 reduce-scatter.7
  579.6 31.6 reduce-scatter.9
where the time goes:
time: 637 us; the launch traced here: 636 us
  waiting for transfers between devices  452 us (71%)
  blocking collectives  114 us (18%)
  matrix products  32.1 us (5%)
  between operations  15.7 us (2%)
  other arithmetic  14.4 us (2%)
  local copies, waits for them, and re-layouts  8.34 us (1%)
    reduce_scatter x1, waiting for transfers between devices, on_device(): lax.psum_scatter(lax.dot_general(part_a, view_b_all, (((0,), (0,)), ((),...  280 us
    all_gather x1, waiting for transfers between devices, on_device(): piece = lax.all_gather(grad_corr, 'dp', axis=0, tiled=True)  123 us
    psum x1, blocking collectives, on_device(): loss_value = lax.psum(loss_part, ('dp', 'mp')) / float(full_width)  46.6 us
    psum x1, blocking collectives, on_device(): lax.psum((jnp.sum(grads, axis=1), jnp.sum(grads * normed, axis=1)), 'dp')  29.9 us
    reduce_scatter x1, waiting for transfers between devices, on_device(): lax.psum_scatter(grad_part.astype(jnp.bfloat16), 'mp', scatter_dimension=...  25.2 us
    all_gather x1, waiting for transfers between devices, on_device(): view_b_all = lax.all_gather(embed[1], 'mp', axis=1, tiled=True)  23.6 us
    psum x1, blocking collectives, on_device(): spread = lax.psum(jnp.sum(centred * centred, axis=1), 'dp') / batch_all  21.6 us
    psum x1, blocking collectives, on_device(): mean = lax.psum(jnp.sum(pre, axis=1), 'dp') / batch_all  15.4 us
  transfers between devices with their start and end apart: 5, of which 4 were waited for; matrix products, arithmetic and copies ran while one was open for 1% of the time, Pallas kernels for 0%

commit v1 on v0

v1 whole, which is shorter than its diff:
```python
import functools

import jax
import jax.numpy as jnp
from jax import lax
from jax.sharding import PartitionSpec as P

BF = jnp.bfloat16
F32 = jnp.float32


def lanes(parts):
    flat = jnp.concatenate([p.reshape(-1) for p in parts])
    return jnp.pad(flat, (0, -flat.shape[0] % 1024)).reshape(-1, 128)


def on_device(n, n_mp, features, proj_weight):
    rows, d_in = features.shape[1:]
    width = proj_weight.shape[1]
    part = d_in // n_mp
    batch = float(rows * n)
    few = float(rows)
    m = lax.axis_index("mp")

    flat = features.reshape(2 * rows, d_in)
    pre = jnp.dot(flat, proj_weight, preferred_element_type=F32).reshape(2, rows, width)
    f_mean = jnp.mean(features.astype(F32), axis=1)
    p_mean = jnp.mean(pre, axis=1)
    near = pre - p_mean[:, None, :]
    squares = jnp.sum(near * near, axis=1)
    cross = jnp.sum(near[0] * near[1], axis=0)
    stats = lax.all_gather(lanes([f_mean, p_mean, squares, cross]), "dp")
    stats = stats.reshape(n, -1)
    cuts = [2 * d_in, 2 * d_in + 2 * width, 2 * d_in + 4 * width]
    f_means = stats[:, : cuts[0]].reshape(n, 2, d_in)
    p_means = stats[:, cuts[0] : cuts[1]].reshape(n, 2, width)
    all_squares = stats[:, cuts[1] : cuts[2]].reshape(n, 2, width)
    all_cross = stats[:, cuts[2] : cuts[2] + width]
    f_all = jnp.mean(f_means, axis=0)
    mean = jnp.mean(p_means, axis=0)
    off = p_means - mean
    spread = (jnp.sum(all_squares, axis=0) + few * jnp.sum(off * off, axis=0)) / batch
    scale = lax.rsqrt(spread + 1e-05)
    corr_diag = (
        (jnp.sum(all_cross, axis=0) + few * jnp.sum(off[:, 0] * off[:, 1], axis=0)) / batch * scale[0] * scale[1]
    )
    extra = (2.0 - 2.0 * 0.0051) * corr_diag - 2.0

    f_a = lax.dynamic_slice_in_dim(features[0], m * part, part, 1)
    ma_here = lax.dynamic_slice_in_dim(f_mean[0], m * part, part, 0)
    ma_all = lax.dynamic_slice_in_dim(f_all[0], m * part, part, 0)
    outer = few * (
        ma_here[:, None] * f_mean[1][None, :]
        - (ma_here - ma_all)[:, None] * (f_mean[1] - f_all[1])[None, :]
    )
    sig = lax.dot_general(f_a, features[1], (((0,), (0,)), ((), ())), preferred_element_type=F32) - outer
    sig = lax.psum_scatter(sig / batch, "dp", scatter_dimension=0, tiled=True).astype(BF)

    centred = pre - mean[:, None, :]
    normed = centred * scale[:, None, :]
    embed = normed.astype(BF)
    scaled = (normed * scale[:, None, :]).astype(BF).reshape(2 * rows, width)
    u = lax.dot_general(scaled, proj_weight, (((1,), (1,)), ((), ())), preferred_element_type=F32)
    u = lax.psum(u.astype(BF), "mp")
    sig = lax.all_gather(sig, ("mp", "dp"), axis=0, tiled=True)

    v_a = lax.dot_general(u[rows:], sig, (((1,), (1,)), ((), ())), preferred_element_type=F32).astype(BF)
    v_b = jnp.dot(u[:rows], sig, preferred_element_type=F32).astype(BF)
    h = jnp.dot(jnp.concatenate([v_a, v_b]), proj_weight, preferred_element_type=F32)
    h = h.reshape(2, rows, width) * scale[:, None, :]
    grads = 2.0 * 0.0051 * h + extra * embed[::-1].astype(F32)
    first = jnp.sum(grads, axis=1)
    second = jnp.sum(grads * normed, axis=1)
    row_squares = jnp.sum(h[0] * normed[0], axis=0)
    sums = lax.psum(lanes([first, second, row_squares]), "dp").reshape(-1) / batch
    first = sums[: 2 * width].reshape(2, width)
    second = sums[2 * width : 4 * width].reshape(2, width)
    row_squares = sums[4 * width : 5 * width]
    loss_part = jnp.sum((1.0 - corr_diag) ** 2 + 0.0051 * (row_squares - corr_diag**2))
    pre_grad = (scale[:, None, :] * (grads - first[:, None, :] - normed * second[:, None, :])).astype(BF)
    pre_grad = pre_grad.reshape(2 * rows, width)
    back = lax.dot_general(pre_grad, proj_weight, (((1,), (1,)), ((), ())), preferred_element_type=F32)
    back = lax.psum_scatter(back.astype(BF), "mp", scatter_dimension=1, tiled=True)
    loss_value = lax.psum(loss_part, "mp") / float(width * n_mp)
    feature_grad = back.reshape(2, rows, part)
    return loss_value, feature_grad


def solution(mesh):
    placed = (P(None, "dp", None), P(None, "mp"))
    return jax.shard_map(
        functools.partial(on_device, mesh.shape["dp"], mesh.shape["mp"]),
        mesh=mesh,
        in_specs=placed,
        out_specs=(P(), P(None, "dp", "mp")),
        check_vma=False,
    )
```

time: 637 us -> 279 us (0.44)
  waiting for transfers between devices: 452 us -> 154 us
  blocking collectives: 114 us -> 63.1 us
  matrix products: 32.1 us -> 19.9 us
    reduce_scatter x2 -> x1, waiting for transfers between devices: 306 us -> 64.7 us  [on_device(): lax.psum_scatter(sig / batch, 'dp', scatter_dimension=0, tiled=True)]
    all_gather x2 -> x1, waiting for transfers between devices: 146 us -> 65.5 us  [on_device(): sig = lax.all_gather(sig, ('mp', 'dp'), axis=0, tiled=True)]
    psum x4 -> x2, blocking collectives: 114 us -> 34.7 us  [the longest x1 28.5 us: on_device(): lax.psum(lanes([first, second, row_squares]), 'dp').reshape(-1) / batch]
    all_gather x0 -> x1, blocking collectives: none -> 28.4 us  [on_device(): stats = lax.all_gather(lanes([f_mean, p_mean, squares, cross]), 'dp')]
    unnamed x6 -> x5, waiting for transfers between devices: 0.1 us -> 24.1 us
    dot_general x5 -> x7, matrix products: 32.1 us -> 19.9 us  [the longest x1 4.1 us: on_device(): v_b = jnp.dot(u[:rows], sig, preferred_element_type=F32).astype(BF)]
  transfers between devices with their start and end apart: 5 -> 4, of which waited for: 4 -> 3; matrix products, arithmetic and copies ran while one was open for 1% -> 3% of each run, Pallas kernels for 0% -> 0%
where the time goes in v1:
time: 279 us; the launch traced here: 277 us
  waiting for transfers between devices  154 us (55%)
  blocking collectives  63.1 us (23%)
  matrix products  19.9 us (7%)
  between operations  17.5 us (6%)
  other arithmetic  12.4 us (4%)
  local copies, waits for them, and re-layouts  9.65 us (3%)
    all_gather x1, waiting for transfers between devices, on_device(): sig = lax.all_gather(sig, ('mp', 'dp'), axis=0, tiled=True)  65.5 us
    reduce_scatter x1, waiting for transfers between devices, on_device(): lax.psum_scatter(sig / batch, 'dp', scatter_dimension=0, tiled=True)  64.7 us
    psum x1, blocking collectives, on_device(): lax.psum(lanes([first, second, row_squares]), 'dp').reshape(-1) / batch  28.5 us
    all_gather x1, blocking collectives, on_device(): stats = lax.all_gather(lanes([f_mean, p_mean, squares, cross]), 'dp')  28.4 us
    unnamed x5, waiting for transfers between devices  24.1 us
    unnamed x23, local copies, waits for them, and re-layouts  8.6 us
    psum x1, blocking collectives, on_device(): loss_value = lax.psum(loss_part, 'mp') / float(width * n_mp)  6.27 us
  transfers between devices with their start and end apart: 4, of which 3 were waited for; matrix products, arithmetic and copies ran while one was open for 3% of the time, Pallas kernels for 0%

profile of v1, /device:TPU:12, one launch (start us, length us, event | category | flops | bytes accessed | tf_op | source)
XLA Modules:
  0.0 277.1 jit_solution(6406295831326017268)
XLA Ops:
  8.0 0.0 copy-start
  8.0 0.0 reduce-scatter.5.cloned.1.call-start
  8.1 0.0 copy-start.6
  8.1 1.8 convert_reduce_fusion
  9.9 0.2 copy-done.6
  10.1 0.9 slice.91
  11.1 0.0 copy-done
  11.1 3.2 %fusion.27 = (f32[2,1024]{1,0:T(2,128)S(1)}, f32[2,256,1024]{2,1,0:T(8,128)S(1)}) fusion(bf16[2,256,1536]{2,1,0:T(8,128)(2,1)} %param.2, bf16[1536,1024]{1,0:T(8,128)(2,1)S(1)} %copy-done), kind=kOutput, calls=%fused_computation.71 | convolution fusion | flops 1611134976 | bytes 6823936 | tf_op jit(solution)/shard_map/dot_general | solution.py:26
  14.3 0.0 copy-start.5
  14.3 0.5 multiply_reduce_fusion.1
  14.8 0.8 copy-done.5
  15.6 0.1 fusion.8
  15.7 28.4 %all_gather.6 = f32[8,64,128]{2,1,0:T(8,128)S(1)} all-gather(f32[1,64,128]{2,1,0:T(8,128)S(1)} %maximum_bitcast_fusion), channel_id=1, replica_groups=mesh['dp'=8,'mp'=4] {'dp'}, dimensions={0}, use_global_device_ids=true | all-gather | bytes 294912 | tf_op jit(solution)/shard_map/all_gather | solution.py:32
  44.1 0.2 copy.16
  44.4 0.1 dynamic-slice_subtract_fusion
  44.5 3.3 %fusion.2 = f32[384,1536]{1,0:T(8,128)} fusion(f32[1536]{0:T(1024)S(1)} %get-tuple-element.7, f32[384]{0:T(512)S(1)} %dynamic-slice_subtract_fusion, f32[1536]{0:T(1024)S(1)} %get-tuple-element.6, f32[384]{0:T(512)S(1)} %dynamic-slice_reduce_fusion, bf16[2,256,1536]{2,1,0:T(8,128)(2,1)} %param.2, bf16[1,256,1536]{2,1,0:T(8,128)(2,1)} %slice.91, s32[]{:T(128)S(6)} %select_n.2), kind=kOutput, calls=%fused_computation.4 | convolution fusion | flops 305528832 | bytes 3357700 | tf_op jit(solution)/shard_map/dot_general | solution.py:56
  47.8 0.0 reduce-scatter.5.cloned.1.call-update
  47.8 0.0 all-reduce.2.cloned.1.call-start
  48.0 3.0 %fusion.24 = (bf16[2,256,1024]{2,1,0:T(8,128)(2,1)}, f32[2,256,1024]{2,1,0:T(8,128)S(1)}) fusion(f32[2,1024]{1,0:T(2,128)S(1)} %reshape.168, f32[2,256,1024]{2,1,0:T(8,128)} %copy-done.5, f32[2,1024]{1,0:T(2,128)S(1)} %div.61), kind=kLoop, calls=%fused_computation.68 | loop fusion | flops 1572864 | bytes 5259264 | tf_op jit(solution)/shard_map/convert_element_type | solution.py:61
  50.9 1.4 copy-done.1
  52.3 0.3 multiply_convert_fusion.1
  52.6 3.1 %convolution_convert_fusion.1 = bf16[512,1536]{1,0:T(8,128)(2,1)} fusion(bf16[512,1024]{1,0:T(8,128)(2,1)S(1)} %bitcast.65, bf16[1536,1024]{1,0:T(8,128)(2,1)S(1)} %copy-done), kind=kOutput, calls=%fused_computation.6 | convolution fusion | flops 1611399168 | bytes 5767168 | tf_op jit(solution)/shard_map/dot_general | solution.py:63
  55.7 0.0 all-reduce.2.cloned.1.call-update
  55.7 0.0 all-gather.2.cloned.1.call-start
  55.7 64.7 %reduce-scatter.5.cloned.1.call-done = f32[48,1536]{1,0:T(8,128)} async-done(((f32[384,1536]{1,0:T(8,128)}), f32[48,1536]{1,0:T(8,128)}) %reduce-scatter.5.cloned.1.call-update) | async-done | bytes 294928 | tf_op jit(solution)/shard_map/reduce_scatter | solution.py:57
  120.5 1.6 convert_element_type.33
  122.1 0.0 all-gather.2.cloned.1.call-update
  122.1 0.0 reduce-scatter.7.cloned.1.call-start
  122.2 0.0 all-reduce.2.cloned.1.call-done
  122.3 65.5 %all-gather.2.cloned.1.call-done = bf16[1536,1536]{1,0:T(8,128)(2,1)} async-done(((bf16[48,1536]{1,0:T(8,128)(2,1)}), bf16[1536,1536]{1,0:T(8,128)(2,1)}) %all-gather.2.cloned.1.call-update) | async-done | bytes 4718608 | tf_op jit(solution)/shard_map/all_gather | solution.py:65
  187.8 4.1 %convolution_convert_fusion.2 = bf16[256,1536]{1,0:T(8,128)(2,1)S(1)} fusion(bf16[1536,1536]{1,0:T(8,128)(2,1)} %all-gather.2.cloned.1.call-done, bf16[512,1536]{1,0:T(8,128)(2,1)} %all-reduce.2.cloned.1.call-done), kind=kOutput, calls=%fused_computation.7 | convolution fusion | flops 1208352768 | bytes 6291456 | tf_op jit(solution)/shard_map/dot_general | solution.py:68
  191.9 0.0 copy-done.7
  191.9 0.3 copy-done.8
  192.2 1.4 convolution_convert_fusion.3
  193.7 1.8 fusion.3
  195.5 0.0 copy-done.4
  195.5 0.8 fusion.15
  196.4 0.2 fusion.7
  196.5 1.1 copy-done.3
  197.7 28.5 %psum.22 = f32[40,128]{1,0:T(8,128)S(1)} all-reduce(f32[40,128]{1,0:T(8,128)S(1)} %maximum_bitcast_fusion.1), channel_id=1, replica_groups=mesh['dp'=8,'mp'=4] {'dp'}, use_global_device_ids=true, to_apply=%region_15.16 | all-reduce | flops 5120 | bytes 40960 | tf_op jit(solution)/shard_map/psum | solution.py:75
  226.2 3.2 %multiply_convert_fusion = bf16[2,256,1024]{2,1,0:T(8,128)(2,1)S(1)} fusion(f32[2,256,1024]{2,1,0:T(8,128)} %copy-done.1, f32[2,1024]{1,0:T(2,128)S(1)} %mul.198, f32[2,1024]{1,0:T(2,128)S(1)} %sub.88, f32[2,1024]{1,0:T(2,128)S(1)} %reshape.168, bf16[2,256,1024]{2,1,0:T(8,128)(2,1)} %get-tuple-element.11, f32[1024]{0:T(1024)S(1)} %get-tuple-element.9, ...), kind=kLoop, calls=%fused_computation.9 | loop fusion | flops 4718592 | bytes 6320128 | tf_op jit(solution)/shard_map/convert_element_type | solution.py:80
  229.4 3.0 %convolution_convert_fusion = bf16[512,1536]{1,0:T(8,128)(2,1)} fusion(bf16[512,1024]{1,0:T(8,128)(2,1)S(1)} %bitcast.67, bf16[1536,1024]{1,0:T(8,128)(2,1)S(1)} %copy-done), kind=kOutput, calls=%fused_computation.5 | convolution fusion | flops 1611399168 | bytes 5767168 | tf_op jit(solution)/shard_map/dot_general | solution.py:82
  232.4 2.6 copy.4
  235.0 0.0 reduce-scatter.7.cloned.1.call-update
  235.0 0.6 fusion.20
  235.6 6.3 %psum.23 = f32[]{:T(128)} all-reduce(f32[]{:T(128)} %fusion.20), channel_id=1, replica_groups=mesh['dp'=8,'mp'=4] {'mp'}, use_global_device_ids=true, to_apply=%region_17.18 | all-reduce | flops 1 | bytes 8 | tf_op jit(solution)/shard_map/psum | solution.py:84
  242.6 24.0 %reduce-scatter.7.cloned.1.call-done = bf16[384,512]{1,0:T(8,128)(2,1)} async-done(((bf16[1536,512]{1,0:T(8,128)(2,1)}), bf16[384,512]{1,0:T(8,128)(2,1)}) %reduce-scatter.7.cloned.1.call-update) | async-done | bytes 393232
  266.6 1.9 copy.5
  (34 shorter events, 0.3 us)
Async XLA Ops:
  8.0 3.1 %copy-start = (bf16[1536,1024]{1,0:T(8,128)(2,1)S(1)}, bf16[1536,1024]{1,0:T(8,128)(2,1)}, u32[]{:S(2)}) copy-start(bf16[1536,1024]{1,0:T(8,128)(2,1)} %param.3) | copy-start | bytes 9437188
  8.0 112.4 %reduce-scatter.5.cloned.1.call-start = ((), (), s32[]{:S(2)}) async-start(), calls=%async_computation.3 | async-start | bytes 2654208 | tf_op jit(solution)/shard_map/reduce_scatter | solution.py:57
  8.1 2.0 copy-start.6
  14.3 1.3 copy-start.5
  47.8 74.5 %all-reduce.2.cloned.1.call-start = ((), (), s32[]{:S(2)}) async-start(), calls=%async_computation.2 | async-start | bytes 3145728 | tf_op jit(solution)/shard_map/psum | solution.py:64
  50.9 1.4 copy-start.1
  55.7 132.1 %all-gather.2.cloned.1.call-start = ((), (), s32[]{:S(2)}) async-start(), calls=%async_computation.4 | async-start | bytes 4866048 | tf_op jit(solution)/shard_map/all_gather | solution.py:65
  122.1 144.5 %reduce-scatter.7.cloned.1.call-start = ((), (), s32[]{:S(2)}) async-start(), calls=%async_computation.5 | async-start | bytes 1966080
  187.8 4.1 %copy-start.7 = (bf16[1536,1536]{1,0:T(8,128)(2,1)S(1)}, bf16[1536,1536]{1,0:T(8,128)(2,1)}, u32[]{:S(2)}) copy-start(bf16[1536,1536]{1,0:T(8,128)(2,1)} %all-gather.2.cloned.1.call-done) | copy-start | bytes 14155780
  187.8 4.5 %copy-start.8 = (bf16[512,1536]{1,0:T(8,128)(2,1)S(1)}, bf16[512,1536]{1,0:T(8,128)(2,1)}, u32[]{:S(2)}) copy-start(bf16[512,1536]{1,0:T(8,128)(2,1)} %all-reduce.2.cloned.1.call-done) | copy-start | bytes 4718596
  193.6 1.8 copy-start.2
  193.6 1.8 copy-start.4
  196.3 1.4 copy-start.3
Sparse Core Ops, SparseCore 0:
  47.9 72.4 reduce-scatter.4
  123.9 63.7 all-gather.1
Sparse Core Ops, SparseCore 1:
  55.8 46.2 all-reduce.1
  235.1 31.4 reduce-scatter.6
